TPU v7x, 256 devices: a whole 4x4x8 slice. The times are simulated.
256 devices in a mesh: pop: 32 (over x, z_lo, core), tensor: 8 (over z_hi, y).
Axes of the slice: x: 4, y: 4, z: 8 (z_hi: 2, z_lo: 4; z = z_hi * 4 + z_lo), core: 2. Of those that a mesh axis runs over, the one named last changes fastest.
Arguments:
- inputs: bfloat16 [64, 384, 4096], P('pop', None, 'tensor'), may hold values from -6 to 6
- readout: bfloat16 [64, 384, 4096], P('pop', None, 'tensor'), may hold values from -6 to 6
- recept_weight: bfloat16 [4096, 4096], P(None, 'tensor'), may hold values from -0.09375 to 0.09375
- output_weight: bfloat16 [4096, 4096], P(None, 'tensor'), may hold values from -0.09375 to 0.09375
- left_vectors: bfloat16 [2, 64, 4096], P(None, 'pop'), may hold values from -6 to 6
- right_vectors: bfloat16 [2, 64, 4096], P(None, 'pop', 'tensor'), may hold values from -6 to 6
- fitness: float32 [64], P('pop'), may hold values from -4 to 4
Outputs:
- outputs: bfloat16 [64, 384, 4096], P('pop', None, 'tensor')
- estimate: float32 [2, 4096, 4096], P(None, 'pop', 'tensor')
All inputs are finite; a program needn't handle non-finite values.
Results may differ from a plain program's by a relative error of at most 0.0049.
Values may be sent and summed in bfloat16 or wider, within the bound.
A program may use at most 128 MiB of HBM per device.

v0:
```python
import jax
import jax.numpy as jnp
from jax import lax
from jax.sharding import PartitionSpec as P

noise_scale = 0.02


def folded_projection(weight, left_local, piece):
    product = jnp.einsum("msn,nc->msc", piece, weight, preferred_element_type=jnp.float32)
    projected = jnp.einsum("msn,mn->ms", piece, left_local, preferred_element_type=jnp.float32)
    return (product, projected)


def local(inputs, readout, recept_weight, output_weight, left_vectors, right_vectors, fitness):
    members, seq_len = (inputs.shape[0], inputs.shape[1])
    pre_r, proj_r = folded_projection(
        recept_weight, left_vectors[0], lax.all_gather(inputs, "tensor", axis=2, tiled=True)
    )
    pre_r = (
        pre_r + noise_scale * proj_r[:, :, None] * right_vectors[0].astype(jnp.float32)[:, None, :]
    )
    gated = (jax.nn.sigmoid(pre_r) * readout.astype(jnp.float32)).astype(jnp.bfloat16)
    pre_o, proj_o = folded_projection(
        output_weight, left_vectors[1], lax.all_gather(gated, "tensor", axis=2, tiled=True)
    )
    pre_o = (
        pre_o + noise_scale * proj_o[:, :, None] * right_vectors[1].astype(jnp.float32)[:, None, :]
    )
    outputs = pre_o.astype(jnp.bfloat16)
    width = left_vectors.shape[2]
    row_count = width // lax.axis_size("pop")
    parts = []
    for which in range(2):

        def weighted_term(start, count, which=which):
            left_part = left_vectors[which].astype(jnp.float32)
            left_part = left_part * fitness[:, None]
            return jnp.dot(
                left_part.T,
                right_vectors[which].astype(jnp.float32),
                precision=lax.Precision.HIGHEST,
            )

        parts.append(
            lax.psum_scatter(
                weighted_term(jnp.int32(0), row_count * lax.axis_size("pop")),
                "pop",
                scatter_dimension=0,
                tiled=True,
            )
        )
    summed = jnp.stack(parts)
    total_members = members * lax.axis_size("pop")
    estimate = summed / (noise_scale * total_members)
    return (outputs, estimate)


def solution(mesh):
    return jax.shard_map(
        local,
        mesh=mesh,
        in_specs=(
            P("pop", None, "tensor"),
            P("pop", None, "tensor"),
            P(None, "tensor"),
            P(None, "tensor"),
            P(None, "pop", None),
            P(None, "pop", "tensor"),
            P("pop"),
        ),
        out_specs=(P("pop", None, "tensor"), P(None, "pop", "tensor")),
        check_vma=False,
    )
```

profile of v0, /device:TPU:24, one launch (start us, length us, event | category | flops | bytes accessed | tf_op | source)
XLA Modules:
  0.0 522.4 jit_solution(8463058563027532059)
XLA Ops:
  8.0 0.0 all-gather.3.cloned.1.call-start
  8.0 0.7 all-gather.3.cloned.1.call-update
  8.7 0.0 reduce-scatter.5.cloned.1.call-start
  8.8 7.5 %fusion.8 = f32[4096,512]{1,0:T(8,128)} fusion(f32[2]{0:T(128)} %param.13, bf16[2,2,4096]{2,1,0:T(2,128)(2,1)} %param.11, bf16[2,2,512]{2,1,0:T(2,128)(2,1)} %param.12), kind=kOutput, calls=%fused_computation.7 | convolution fusion | flops 50348032 | bytes 8407552 | tf_op jit(solution)/shard_map/dot_general | solution.py:39
  16.3 0.0 reduce-scatter.5.cloned.1.call-update
  16.3 0.0 reduce-scatter.3.cloned.1.call-start
  16.3 0.7 copy-done.2
  17.0 0.0 copy-done.3
  17.0 0.0 copy-done.4
  17.0 5.8 %fusion.10 = f32[4096,512]{1,0:T(8,128)} fusion(f32[2]{0:T(128)S(1)} %copy-done.4, bf16[2,2,4096]{2,1,0:T(2,128)(2,1)S(1)} %copy-done.2, bf16[2,2,512]{2,1,0:T(2,128)(2,1)S(1)} %copy-done.3), kind=kOutput, calls=%fused_computation.9 | convolution fusion | flops 50348032 | bytes 8407552 | tf_op jit(solution)/shard_map/dot_general | solution.py:39
  22.8 0.0 reduce-scatter.3.cloned.1.call-update
  22.8 0.2 all-gather.5.cloned.1.call-start
  23.1 115.7 %all-gather.3.cloned.1.call-done = bf16[2,384,4096]{2,1,0:T(8,128)(2,1)} async-done(((bf16[2,384,512]{2,1,0:T(8,128)(2,1)}), bf16[2,384,4096]{2,1,0:T(8,128)(2,1)}) %all-gather.3.cloned.1.call-update) | async-done | bytes 6291472 | tf_op jit(solution)/shard_map/all_gather | solution.py:18
  138.8 4.7 fusion.14
  143.5 0.0 copy-done.5
  143.5 0.0 copy-done
  143.6 6.8 %multiply_convert_fusion = bf16[2,384,512]{2,1,0:T(8,128)(2,1)} fusion(bf16[2,384,512]{2,1,0:T(8,128)(2,1)S(1)} %copy-done.5, bf16[2,384,4096]{2,1,0:T(8,128)(2,1)S(1)} %copy-done, bf16[4096,512]{1,0:T(8,128)(2,1)} %param.9, f32[2,512]{1,0:T(2,128)S(1)} %get-tuple-element.5, f32[2,384]{1,0:T(2,128)S(1)} %bitcast_multiply_fusion.1), kind=kOutput, calls=%fused_computation.5 | convolution fusion | flops 3224371200 | bytes 12065792 | tf_op jit(solution)/shard_map/msn,nc->msc/dot_general | solution.py:10
  150.3 0.0 all-gather.5.cloned.1.call-update
  150.4 187.2 %reduce-scatter.5.cloned.1.call-done = f32[128,512]{1,0:T(8,128)} async-done(((f32[4096,512]{1,0:T(8,128)}), f32[128,512]{1,0:T(8,128)}) %reduce-scatter.5.cloned.1.call-update) | async-done | bytes 262160 | tf_op jit(solution)/shard_map/reduce_scatter | solution.py:46
  337.6 164.4 %reduce-scatter.3.cloned.1.call-done = f32[128,512]{1,0:T(8,128)} async-done(((f32[4096,512]{1,0:T(8,128)}), f32[128,512]{1,0:T(8,128)}) %reduce-scatter.3.cloned.1.call-update) | async-done | bytes 262160 | tf_op jit(solution)/shard_map/reduce_scatter | solution.py:46
  502.0 1.9 maximum_multiply_fusion
  503.8 4.7 fusion.12
  508.5 0.0 copy-done.1
  508.5 6.5 %add_convert_fusion = bf16[2,384,512]{2,1,0:T(8,128)(2,1)} fusion(bf16[2,384,4096]{2,1,0:T(8,128)(2,1)S(1)} %copy-done.1, bf16[4096,512]{1,0:T(8,128)(2,1)} %param.10, f32[2,512]{1,0:T(2,128)S(1)} %get-tuple-element.4, f32[2,384]{1,0:T(2,128)S(1)} %bitcast_multiply_fusion), kind=kOutput, calls=%fused_computation.4 | convolution fusion | flops 3222405120 | bytes 11279360 | tf_op jit(solution)/shard_map/msn,nc->msc/dot_general | solution.py:10
  (11 shorter events, 0.1 us)
Async XLA Ops:
  8.0 130.8 %all-gather.3.cloned.1.call-start = ((), (), s32[]{:S(2)}) async-start(), calls=%async_computation.2 | async-start | bytes 7077888 | tf_op jit(solution)/shard_map/all_gather | solution.py:18
  8.7 328.9 %reduce-scatter.5.cloned.1.call-start = ((), (), s32[]{:S(2)}) async-start(), calls=%async_computation.5 | async-start | bytes 8650752 | tf_op jit(solution)/shard_map/reduce_scatter | solution.py:46
  16.3 0.8 copy-start.2
  16.3 0.8 copy-start.3
  16.3 0.8 copy-start.4
  16.3 485.7 %reduce-scatter.3.cloned.1.call-start = ((), (), s32[]{:S(2)}) async-start(), calls=%async_computation.4 | async-start | bytes 8650752 | tf_op jit(solution)/shard_map/reduce_scatter | solution.py:46
  22.8 120.7 %copy-start.5 = (bf16[2,384,512]{2,1,0:T(8,128)(2,1)S(1)}, bf16[2,384,512]{2,1,0:T(8,128)(2,1)}, u32[]{:S(2)}) copy-start(bf16[2,384,512]{2,1,0:T(8,128)(2,1)} %param.8) | copy-start | bytes 2359300
  22.8 481.0 %all-gather.5.cloned.1.call-start = ((), (), s32[]{:S(2)}) async-start(), calls=%async_computation.3 | async-start | bytes 7077888 | tf_op jit(solution)/shard_map/all_gather | solution.py:25
  138.8 4.7 copy-start
  503.8 4.7 copy-start.1
Sparse Core Ops, SparseCore 0:
  11.3 127.4 all-gather.2
  150.5 148.6 all-gather.4
Sparse Core Ops, SparseCore 1:
  16.4 321.1 reduce-scatter.4
  340.0 161.9 reduce-scatter.2
where the time goes:
time: 523 us; the launch traced here: 522 us
  waiting for transfers between devices  468 us (89%)
  matrix products  35.9 us (7%)
  between operations  15.5 us (3%)
    reduce_scatter x2, waiting for transfers between devices, local(): lax.psum_scatter(weighted_term(jnp.int32(0), row_count * lax.axis_size('p...  352 us
    all_gather x1, waiting for transfers between devices, local(): lax.all_gather(inputs, 'tensor', axis=2, tiled=True)  116 us
    dot_general x2, matrix products, folded_projection(): jnp.einsum('msn,nc->msc', piece, weight, preferred_element_type=jnp.float32)  13.3 us
    dot_general x2, matrix products, weighted_term(): jnp.dot(left_part.T, right_vectors[which].astype(jnp.float32), precision=...  13.2 us
  transfers between devices with their start and end apart: 4, of which 3 were waited for; matrix products, arithmetic and copies ran while one was open for 5% of the time, Pallas kernels for 0%

commit v1 on v0

--- a/solution.py
+++ b/solution.py
@@ -28,30 +28,17 @@
         pre_o + noise_scale * proj_o[:, :, None] * right_vectors[1].astype(jnp.float32)[:, None, :]
     )
     outputs = pre_o.astype(jnp.bfloat16)
-    width = left_vectors.shape[2]
-    row_count = width // lax.axis_size("pop")
-    parts = []
-    for which in range(2):
-
-        def weighted_term(start, count, which=which):
-            left_part = left_vectors[which].astype(jnp.float32)
-            left_part = left_part * fitness[:, None]
-            return jnp.dot(
-                left_part.T,
-                right_vectors[which].astype(jnp.float32),
-                precision=lax.Precision.HIGHEST,
-            )
-
-        parts.append(
-            lax.psum_scatter(
-                weighted_term(jnp.int32(0), row_count * lax.axis_size("pop")),
-                "pop",
-                scatter_dimension=0,
-                tiled=True,
-            )
-        )
-    summed = jnp.stack(parts)
     total_members = members * lax.axis_size("pop")
+    left_all = lax.all_to_all(left_vectors, "pop", split_axis=2, concat_axis=1, tiled=True)
+    right_all = lax.all_gather(right_vectors, "pop", axis=1, tiled=True)
+    fitness_all = lax.all_gather(fitness, "pop", axis=0, tiled=True)
+    weighted = left_all.astype(jnp.float32) * fitness_all[None, :, None]
+    summed = jnp.einsum(
+        "kmr,kmc->krc",
+        weighted,
+        right_all.astype(jnp.float32),
+        precision=lax.Precision.HIGHEST,
+    )
     estimate = summed / (noise_scale * total_members)
     return (outputs, estimate)
 

time: 523 us -> 353 us (0.67)
  the two profiles are of different devices: /device:TPU:24 before, /device:TPU:33 now
where the time goes in v1:
time: 353 us; the launch traced here: 351 us
  waiting for transfers between devices  150 us (42%)
  blocking collectives  133 us (38%)
  matrix products  23.9 us (7%)
  local copies, waits for them, and re-layouts  17.9 us (5%)
  between operations  14.7 us (4%)
  starting transfers between devices  7.15 us (2%)
  other arithmetic  4.5 us (1%)
    all_gather x1, waiting for transfers between devices, local(): lax.all_gather(inputs, 'tensor', axis=2, tiled=True)  149 us
    unnamed x1, blocking collectives  68 us
    all_gather x1, blocking collectives, local(): right_all = lax.all_gather(right_vectors, 'pop', axis=1, tiled=True)  65.5 us
    dot_general x2, matrix products, folded_projection(): jnp.einsum('msn,nc->msc', piece, weight, preferred_element_type=jnp.float32)  13.3 us
    unnamed x21, local copies, waits for them, and re-layouts  12 us
    dot_general x2, matrix products, folded_projection(): jnp.einsum('msn,mn->ms', piece, left_local, preferred_element_type=jnp.fl...  9.3 us
    all_to_all x1, starting transfers between devices, local(): lax.all_to_all(left_vectors, 'pop', split_axis=2, concat_axis=1, tiled=True)  7.07 us
  transfers between devices with their start and end apart: 3, of which 1 were waited for; matrix products, arithmetic and copies ran while one was open for 7% of the time, Pallas kernels for 0%

profile of v1, /device:TPU:33, one launch (start us, length us, event | category | flops | bytes accessed | tf_op | source)
XLA Modules:
  0.0 351.3 jit_solution(15353262629847234596)
XLA Ops:
  7.2 0.0 all-gather.3.cloned.1.call-start
  7.2 0.7 all-gather.3.cloned.1.call-update
  7.9 0.0 all-gather.5.cloned.1.call-start
  8.0 0.7 bitcast_convert_fusion
  8.7 0.8 slice_bitcast_fusion
  9.4 149.0 %all-gather.3.cloned.1.call-done = bf16[2,384,4096]{2,1,0:T(8,128)(2,1)} async-done(((bf16[2,384,512]{2,1,0:T(8,128)(2,1)}), bf16[2,384,4096]{2,1,0:T(8,128)(2,1)}) %all-gather.3.cloned.1.call-update) | async-done | bytes 6291472 | tf_op jit(solution)/shard_map/all_gather | solution.py:18
  158.4 4.7 %fusion.12 = f32[2,1,384]{2,1,0:T(1,128)S(1)} fusion(bf16[2,384,4096]{2,1,0:T(8,128)(2,1)} %all-gather.3.cloned.1.call-done, bf16[2,4096,1]{1,0,2:T(2,128)(2,1)S(1)} %get-tuple-element.3), kind=kOutput, calls=%fused_computation.12 | convolution fusion | flops 6291456 | bytes 6310912 | tf_op jit(solution)/shard_map/msn,mn->ms/dot_general | solution.py:11
  163.1 0.0 copy-done.1
  163.1 0.0 copy-start.2
  163.1 6.8 %multiply_convert_fusion = bf16[2,384,512]{2,1,0:T(8,128)(2,1)} fusion(bf16[2,384,512]{2,1,0:T(8,128)(2,1)S(1)} %copy-done.4, bf16[2,384,4096]{2,1,0:T(8,128)(2,1)S(1)} %copy-done.1, bf16[4096,512]{1,0:T(8,128)(2,1)} %param.9, f32[2,512]{1,0:T(2,128)S(1)} %get-tuple-element.5, f32[2,384]{1,0:T(2,128)S(1)} %bitcast_multiply_fusion.1), kind=kOutput, calls=%fused_computation.6 | convolution fusion | flops 3224371200 | bytes 12065792 | tf_op jit(solution)/shard_map/msn,nc->msc/dot_general | solution.py:10
  169.8 0.0 all-gather.5.cloned.1.call-update
  169.9 2.8 copy.10
  172.7 3.8 %reshape.42 = bf16[32,2,256]{2,1,0:T(2,128)(2,1)} reshape(bf16[4096,2,2]{2,1,0:T(2,128)(2,1)S(1)} %bitcast.39) | data formatting | bytes 65536
  176.5 7.1 %all-to-all-start = ((bf16[32,2,256]{2,1,0:T(2,128)(2,1)}), bf16[32,2,256]{2,1,0:T(2,128)(2,1)S(1)}, u32[]{:S(2)}, u32[]{:S(2)}) async-start(bf16[32,2,256]{2,1,0:T(2,128)(2,1)} %reshape.42), calls=%async_computation | async-start | bytes 65536 | tf_op jit(solution)/shard_map/all_to_all | solution.py:32
  183.6 0.6 dynamic-slice
  184.8 0.2 dynamic-update-slice
  185.0 68.0 %all-reduce = f32[64]{0:T(128)S(1)} all-reduce(f32[64]{0:T(128)S(1)} %dynamic-update-slice), channel_id=1, replica_groups=mesh['pop'=32,'tensor'=8] {'pop'}, use_global_device_ids=true, to_apply=%add | all-reduce | flops 64 | bytes 512
  253.0 65.5 %all_gather.15 = bf16[2,64,512]{2,0,1:T(2,128)(2,1)S(1)} all-gather(bf16[2,2,512]{2,0,1:T(2,128)(2,1)S(1)} %copy.12), channel_id=1, replica_groups=mesh['pop'=32,'tensor'=8] {'pop'}, dimensions={1}, use_global_device_ids=true | all-gather | bytes 135168 | tf_op jit(solution)/shard_map/all_gather | solution.py:33
  318.5 4.5 %reshape.43 = bf16[4096,2,2]{2,1,0:T(2,128)(2,1)S(1)} reshape(bf16[32,2,256]{2,1,0:T(2,128)(2,1)S(1)} %all-to-all-done) | data formatting | bytes 65536
  323.1 3.8 %convert_bitcast_fusion = f32[2,32,2,128]{2,0,3,1:T(2,128)} fusion(bf16[2,2,32,128]{1,0,3,2:T(2,128)(2,1)S(1)} %bitcast.38), kind=kLoop, calls=%fused_computation | loop fusion | flops 16384 | bytes 98304 | tf_op jit(solution)/shard_map/convert_element_type | solution.py:35
  326.9 5.2 %copy.11 = f32[2,32,2,128]{3,2,1,0:T(2,128)S(1)} copy(f32[2,32,2,128]{2,0,3,1:T(2,128)} %convert_bitcast_fusion) | data formatting | bytes 131072 | tf_op jit(solution)/shard_map/convert_element_type | solution.py:35
  332.0 1.3 convolution_multiply_fusion
  333.3 4.7 %fusion.10 = f32[2,1,384]{2,1,0:T(1,128)S(1)} fusion(bf16[2,384,4096]{2,1,0:T(8,128)(2,1)} %all-gather.5.cloned.1.call-done, bf16[2,4096,1]{1,0,2:T(2,128)(2,1)S(1)} %get-tuple-element.2), kind=kOutput, calls=%fused_computation.10 | convolution fusion | flops 6291456 | bytes 6310912 | tf_op jit(solution)/shard_map/msn,mn->ms/dot_general | solution.py:11
  338.0 6.5 %add_convert_fusion = bf16[2,384,512]{2,1,0:T(8,128)(2,1)} fusion(bf16[2,384,4096]{2,1,0:T(8,128)(2,1)S(1)} %copy-done, bf16[4096,512]{1,0:T(8,128)(2,1)} %param.10, f32[2,512]{1,0:T(2,128)S(1)} %get-tuple-element.4, f32[2,384]{1,0:T(2,128)S(1)} %bitcast_multiply_fusion), kind=kOutput, calls=%fused_computation.5 | convolution fusion | flops 3222405120 | bytes 11279360 | tf_op jit(solution)/shard_map/msn,nc->msc/dot_general | solution.py:10
  (18 shorter events, 0.0 us)
Async XLA Ops:
  7.2 155.9 %copy-start.4 = (bf16[2,384,512]{2,1,0:T(8,128)(2,1)S(1)}, bf16[2,384,512]{2,1,0:T(8,128)(2,1)}, u32[]{:S(2)}) copy-start(bf16[2,384,512]{2,1,0:T(8,128)(2,1)} %param.8) | copy-start | bytes 2359300
  7.2 151.2 %all-gather.3.cloned.1.call-start = ((), (), s32[]{:S(2)}) async-start(), calls=%async_computation.1 | async-start | bytes 7077888 | tf_op jit(solution)/shard_map/all_gather | solution.py:18
  7.9 325.4 %all-gather.5.cloned.1.call-start = ((), (), s32[]{:S(2)}) async-start(), calls=%async_computation.2 | async-start | bytes 7077888 | tf_op jit(solution)/shard_map/all_gather | solution.py:25
  158.4 4.7 %copy-start.1 = (bf16[2,384,4096]{2,1,0:T(8,128)(2,1)S(1)}, bf16[2,384,4096]{2,1,0:T(8,128)(2,1)}, u32[]{:S(2)}) copy-start(bf16[2,384,4096]{2,1,0:T(8,128)(2,1)} %all-gather.3.cloned.1.call-done) | copy-start | bytes 18874372
  163.1 6.8 %copy-start.2 = (bf16[2,2,4096]{2,1,0:T(2,128)(2,1)S(1)}, bf16[2,2,4096]{2,1,0:T(2,128)(2,1)}, u32[]{:S(2)}) copy-start(bf16[2,2,4096]{2,1,0:T(2,128)(2,1)} %param.11) | copy-start | bytes 98308
  169.8 13.8 %copy-start.3 = (bf16[2,2,512]{2,1,0:T(2,128)(2,1)S(1)}, bf16[2,2,512]{2,1,0:T(2,128)(2,1)}, u32[]{:S(2)}) copy-start(bf16[2,2,512]{2,1,0:T(2,128)(2,1)} %param.12) | copy-start | bytes 12292
  169.8 13.8 %copy-start.6 = (u32[256]{0:T(256)S(1)}, u32[256]{0:T(256)}, u32[]{:S(2)}) copy-start(u32[256]{0:T(256)} %constant.14) | copy-start | bytes 3076
  169.8 14.9 %copy-start.5 = (f32[2]{0:T(128)S(1)}, f32[2]{0:T(128)}, u32[]{:S(2)}) copy-start(f32[2]{0:T(128)} %param.13) | copy-start | bytes 28
  176.5 142.0 %all-to-all-start = ((bf16[32,2,256]{2,1,0:T(2,128)(2,1)}), bf16[32,2,256]{2,1,0:T(2,128)(2,1)S(1)}, u32[]{:S(2)}, u32[]{:S(2)}) async-start(bf16[32,2,256]{2,1,0:T(2,128)(2,1)} %reshape.42), calls=%async_computation | async-start | bytes 65536 | tf_op jit(solution)/shard_map/all_to_all | solution.py:32
  333.3 4.7 %copy-start = (bf16[2,384,4096]{2,1,0:T(8,128)(2,1)S(1)}, bf16[2,384,4096]{2,1,0:T(8,128)(2,1)}, u32[]{:S(2)}) copy-start(bf16[2,384,4096]{2,1,0:T(8,128)(2,1)} %all-gather.5.cloned.1.call-done) | copy-start | bytes 18874372
Sparse Core Ops, SparseCore 0:
  10.5 147.8 all-gather.2
  170.0 144.9 all-gather.4

commit v2 on v1

v2 whole, which is shorter than its diff:
```python
import jax
import jax.numpy as jnp
from jax import lax
from jax.experimental import pallas as pl
from jax.experimental.pallas import tpu as pltpu
from jax.sharding import PartitionSpec as P

MESH = pl.DeviceIdType.MESH
noise_scale = 0.02
CHUNKS = 4
SUBS = 2
F32 = jnp.float32
BF16 = jnp.bfloat16


def mod(value, size):
    return lax.rem(value + size, size)


def device(x, y, z, core):
    return ((x * 4 + lax.rem(z, 4)) * 2 + core, (z // 4) * 4 + y)


def kernel(
    x_hbm, ro_hbm, wr_hbm, wo_hbm, a_hbm, b_hbm, l_hbm, r_hbm,
    out_hbm, est_hbm,
    xg, gg, ro, wr, wo, av, bv, part_out, part_in, outs,
    l1, r1, l2, r2, l3, r3, est,
    xy_s, xy_r, gy_s, gy_r, swap_s, swap_r, wz_s, wz_r, wx_s, wx_r,
    load, part_s, part_r, e1_s, e1_r, e2_s, e2_r, e3_s, e3_r,
):
    pop, tensor = lax.axis_index("pop"), lax.axis_index("tensor")
    x, zl, core = pop // 8, lax.rem(pop // 2, 4), lax.rem(pop, 2)
    zh, y = tensor // 4, lax.rem(tensor, 4)
    z = zh * 4 + zl
    rows, width = ro.shape
    half = xg.shape[1]
    step = rows // CHUNKS
    mover = core != zh
    stays = core == zh

    up, down = device(x, mod(y + 1, 4), z, core), device(x, mod(y + 3, 4), z, core)
    partner = device(x, y, mod(z + 4, 8), 1 - core)
    twin = device(x, y, z, 1 - core)
    z_next = (device(x, y, mod(z + 7, 8), core), device(x, y, mod(z + 1, 8), core))
    x_peer = [device(mod(x + d, 4), y, z, core) for d in range(1, 4)]
    zl_peer = [device(x, y, zh * 4 + mod(zl + d, 4), core) for d in range(1, 4)]
    z_near = [device(x, y, mod(z + d, 8), core) for d in (1, 2, 3, 5, 6, 7)]

    pending = []

    def remote(src, dst, send, recv, target, when=None):
        copy = pltpu.make_async_remote_copy(
            src_ref=src, dst_ref=dst, send_sem=send, recv_sem=recv,
            device_id=target, device_id_type=MESH,
        )
        pending.append((when, copy))
        if when is None:
            copy.start()
        else:
            pl.when(when)(copy.start)

    def arrived(dst, recv):
        pltpu.make_async_remote_copy(
            src_ref=dst, dst_ref=dst, send_sem=recv, recv_sem=recv,
            device_id=twin, device_id_type=MESH,
        ).wait_recv()

    def chunk(k, part=None):
        if part is None:
            return pl.ds(k * step, step)
        return pl.ds(k * step + part * (step // 2), step // 2)

    def columns(which):
        return pl.ds(pl.multiple_of(which * width, width), width)

    mine = columns(y)
    below, above, far = columns(mod(y + 3, 4)), columns(mod(y + 1, 4)), columns(mod(y + 2, 4))
    my_half = pl.ds(pl.multiple_of(core * half, half), half)
    twin_half = pl.ds(pl.multiple_of((1 - core) * half, half), half)

    local = []

    def local_copy(src, dst, sem, when=None):
        copy = pltpu.make_async_copy(src, dst, sem)
        if when is None:
            copy.start()
        else:
            pl.when(when)(copy.start)
        return copy

    load_wr = local_copy(wr_hbm.at[my_half], wr.at[zh], load.at[0])
    load_l = local_copy(l_hbm.at[pl.ds(4 * x, 4)], l1.at[0], load.at[1])
    load_r = local_copy(r_hbm, r1.at[0], load.at[2])
    load_x = [
        local_copy(x_hbm.at[chunk(k)], xg.at[chunk(k), mine], load.at[4 + k], stays)
        for k in range(CHUNKS)
    ]
    load_ro = local_copy(ro_hbm, ro, load.at[8], stays)
    load_a = local_copy(a_hbm.at[:, my_half], av.at[pl.ds(0, 16)], load.at[9], stays)
    load_b = local_copy(b_hbm, bv, load.at[10], stays)
    load_wo = local_copy(wo_hbm.at[my_half], wo.at[zh], load.at[3])
    av[16:, :] = jnp.zeros((av.shape[0] - 16, half), BF16)

    barrier = pltpu.get_barrier_semaphore()
    peers = [up, down, partner, twin] + x_peer + z_near
    for peer in peers:
        pl.semaphore_signal(barrier, inc=1, device_id=peer, device_id_type=MESH)
    pl.semaphore_wait(barrier, len(peers))

    quarter = half // 4
    sub = quarter // (2 * SUBS)

    def weight_rows(direction, j, base=0):
        return pl.ds(
            pl.multiple_of(base + x * quarter + direction * (quarter // 2) + j * sub, sub), sub
        )

    def weight_start(w, hbm, buf):
        for j in range(SUBS):
            for direction, edge in ((0, zl == 0), (1, zl == 3)):
                remote(
                    hbm.at[weight_rows(direction, j, core * half)],
                    buf.at[zh, weight_rows(direction, j)],
                    wz_s.at[w, direction, j, 0], wz_r.at[w, direction, j], z_next[direction], edge,
                )

    relays = []

    def weight_relay(w, buf, slot):
        for j in range(SUBS):
            for direction, hops, last in ((0, 4 - zl, zl == 0), (1, zl + 1, zl == 3)):
                if not 0 < slot - j < 5:
                    continue
                place = buf.at[1 - zh, weight_rows(direction, j)]
                copies = [
                    pltpu.make_async_remote_copy(
                        src_ref=place, dst_ref=place,
                        send_sem=wx_s.at[w, direction, j, d], recv_sem=wx_r.at[w, direction, j, d],
                        device_id=x_peer[d], device_id_type=MESH,
                    )
                    for d in range(3)
                ]
                onward = pltpu.make_async_remote_copy(
                    src_ref=place, dst_ref=place,
                    send_sem=wz_s.at[w, direction, j, 1], recv_sem=wz_r.at[w, direction, j],
                    device_id=z_next[direction], device_id_type=MESH,
                )
                now = hops + j == slot

                @pl.when(now)
                def _(place=place, copies=copies, onward=onward, last=last, w=w, direction=direction, j=j):
                    arrived(place, wz_r.at[w, direction, j])
                    pl.when(jnp.logical_not(last))(onward.start)
                    for copy in copies:
                        copy.start()

                if slot == j + 1:
                    pending.extend((None, copy) for copy in copies)
                    pending.append((jnp.logical_not(last), onward))

    def weight_done(w, buf, loaded):
        for j in range(SUBS):
            for direction in range(2):
                for d in range(3):
                    start = mod(x + 3 - d, 4) * quarter + direction * (quarter // 2) + j * sub
                    arrived(
                        buf.at[1 - zh, pl.ds(pl.multiple_of(start, sub), sub)],
                        wx_r.at[w, direction, j, d],
                    )
        loaded.wait()

    def spread(buf, k, send, recv):
        place = buf.at[chunk(k), mine]
        remote(place, place, send.at[k, 0], recv.at[k, 0], up)
        remote(place, place, send.at[k, 1], recv.at[k, 1], down)

    def relay(buf, k, send, recv):
        arrived(buf.at[chunk(k), below], recv.at[k, 0])
        place = buf.at[chunk(k, 0), below]
        remote(place, place, send.at[k, 2], recv.at[k, 2], up)
        arrived(buf.at[chunk(k), above], recv.at[k, 1])
        place = buf.at[chunk(k, 1), above]
        remote(place, place, send.at[k, 3], recv.at[k, 3], down)

    def gathered(buf, k, recv):
        arrived(buf.at[chunk(k, 0), far], recv.at[k, 2])
        arrived(buf.at[chunk(k, 1), far], recv.at[k, 3])

    def x_ready(k):
        pl.when(stays)(load_x[k].wait)
        pl.when(mover)(lambda: arrived(xg.at[chunk(k), mine], swap_r.at[0, k]))
        spread(xg, k, xy_s, xy_r)

    def project(which, buf, weight, k):
        member = k // (CHUNKS // 2)
        at = which * 2 + member
        slot = which * CHUNKS + k
        value = buf[chunk(k), :]
        theirs = jnp.dot(value, weight[1 - core], preferred_element_type=F32)
        proj = lax.dot_general(
            value, av[...], (((1,), (1,)), ((), ())), preferred_element_type=F32
        )
        part_out[slot, :, :width] = theirs
        part_out[slot, :, width:] = proj
        remote(part_out.at[slot], part_in.at[slot], part_s.at[slot], part_r.at[slot], twin)
        ours = jnp.dot(value, weight[core], preferred_element_type=F32)
        arrived(part_in.at[slot], part_r.at[slot])
        scaled = noise_scale * (proj + part_in[slot, :, width:])[:, at:at + 1]
        return ours + part_in[slot, :, :width] + scaled * bv[at:at + 1, :].astype(F32)

    def first(k):
        gathered(xg, k, xy_r)
        pre = project(0, xg, wr, k)
        if k == 0:
            pl.when(stays)(load_ro.wait)
        pl.when(mover)(lambda: arrived(ro.at[chunk(k)], swap_r.at[1, k]))
        gated = jax.nn.sigmoid(pre) * ro[chunk(k), :].astype(F32)
        gg[chunk(k), mine] = gated.astype(BF16)
        spread(gg, k, gy_s, gy_r)

    store = []

    def second(k):
        gathered(gg, k, gy_r)
        outs[chunk(k), :] = project(1, gg, wo, k).astype(BF16)
        remote(
            outs.at[chunk(k)], out_hbm.at[chunk(k)],
            swap_s.at[2, k], swap_r.at[2, k], partner, mover,
        )
        store.append(local_copy(outs.at[chunk(k)], out_hbm.at[chunk(k)], load.at[11 + k], stays))

    def estimate_one():
        for d in range(3):
            remote(
                l_hbm.at[pl.ds(4 * mod(x + d + 1, 4), 4)], l1.at[d + 1],
                e1_s.at[0, d], e1_r.at[0, d], x_peer[d],
            )
            remote(r_hbm, r1.at[d + 1], e1_s.at[1, d], e1_r.at[1, d], x_peer[d])

    def estimate_two():
        load_l.wait()
        load_r.wait()
        for d in range(3):
            arrived(l1.at[d + 1], e1_r.at[0, d])
            arrived(r1.at[d + 1], e1_r.at[1, d])
        for d in range(3):
            remote(
                l1.at[:, mod(zl + d + 1, 4)], l2.at[d + 1],
                e2_s.at[0, d], e2_r.at[0, d], zl_peer[d],
            )
            remote(r1, r2.at[d + 1], e2_s.at[1, d], e2_r.at[1, d], zl_peer[d])
        l2[0] = l1[:, zl]
        r2[0] = r1[...]

    def estimate_three():
        for d in range(3):
            arrived(l2.at[d + 1], e2_r.at[0, d])
            arrived(r2.at[d + 1], e2_r.at[1, d])
        remote(l2, l3, e3_s.at[0], e3_r.at[0], twin)
        remote(r2, r3, e3_s.at[1], e3_r.at[1], twin)

    def estimate_sum():
        arrived(l3, e3_r.at[0])
        arrived(r3, e3_r.at[1])
        n = 16
        lrow = lax.broadcasted_iota(jnp.int32, (n * 8, n * 16), 0)
        rrow = lax.broadcasted_iota(jnp.int32, (n * 8, n * 16), 1)
        same = (lrow // 8 == rrow // 16) & (lrow % 8 == core * 4 + (rrow % 16) // 4)
        pick = jnp.where(same, 1.0, 0.0).astype(BF16)
        block = lax.broadcasted_iota(jnp.int32, (n * 16, 128), 0) % 4
        which = (lax.broadcasted_iota(jnp.int32, (n * 8, width), 0) // 2) % 2
        total = [None, None]
        for left, right in ((l2, r2), (l3, r3)):
            lv = left[...].reshape(n * 8, 128).T
            rv = right[...].reshape(n * 16, 128).astype(F32)
            wide = jnp.concatenate(
                [jnp.where(block == b, rv, 0.0).astype(BF16) for b in range(width // 128)], axis=1
            )
            chosen = jnp.dot(pick, wide, preferred_element_type=F32)
            high = lv.astype(BF16)
            rest = lv - high.astype(F32)
            middle = rest.astype(BF16)
            low = (rest - middle.astype(F32)).astype(BF16)
            for k in range(2):
                operand = jnp.where(which == k, chosen, 0.0).astype(BF16)
                for piece in (low, middle, high):
                    term = jnp.dot(piece, operand, preferred_element_type=F32)
                    total[k] = term if total[k] is None else total[k] + term
        for k in range(2):
            est[k] = total[k] * (1.0 / (noise_scale * 64))
        store.append(local_copy(est, est_hbm, load.at[15]))

    weight_start(0, wr_hbm, wr)
    remote(b_hbm, bv, swap_s.at[3, 0], swap_r.at[3, 0], partner, mover)
    remote(
        a_hbm.at[:, twin_half], av.at[pl.ds(0, 16)],
        swap_s.at[3, 1], swap_r.at[3, 1], twin, stays,
    )
    estimate_one()
    for k in range(CHUNKS):
        remote(
            x_hbm.at[chunk(k)], xg.at[chunk(k), mine],
            swap_s.at[0, k], swap_r.at[0, k], partner, mover,
        )
    for k in range(CHUNKS):
        remote(
            ro_hbm.at[chunk(k)], ro.at[chunk(k)],
            swap_s.at[1, k], swap_r.at[1, k], partner, mover,
        )
    x_ready(0)
    weight_relay(0, wr, 1)
    estimate_two()
    x_ready(1)
    weight_relay(0, wr, 2)
    relay(xg, 0, xy_s, xy_r)
    estimate_three()
    x_ready(2)
    weight_relay(0, wr, 3)
    relay(xg, 1, xy_s, xy_r)
    estimate_sum()
    weight_relay(0, wr, 4)
    x_ready(3)
    weight_relay(0, wr, 5)
    relay(xg, 2, xy_s, xy_r)
    weight_start(1, wo_hbm, wo)
    relay(xg, 3, xy_s, xy_r)
    pl.when(stays)(lambda: (load_a.wait(), load_b.wait(), None)[2])

    @pl.when(mover)
    def _():
        arrived(av.at[pl.ds(0, 16)], swap_r.at[3, 1])
        arrived(bv, swap_r.at[3, 0])

    weight_done(0, wr, load_wr)
    first(0)
    weight_relay(1, wo, 1)
    first(1)
    weight_relay(1, wo, 2)
    relay(gg, 0, gy_s, gy_r)
    first(2)
    weight_relay(1, wo, 3)
    relay(gg, 1, gy_s, gy_r)
    first(3)
    weight_relay(1, wo, 4)
    relay(gg, 2, gy_s, gy_r)
    weight_relay(1, wo, 5)
    weight_done(1, wo, load_wo)
    second(0)
    relay(gg, 3, gy_s, gy_r)
    for k in range(1, CHUNKS):
        second(k)

    for copy in store[:1]:
        copy.wait()

    @pl.when(stays)
    def _():
        for copy in store[1:]:
            copy.wait()

    @pl.when(mover)
    def _():
        for k in range(CHUNKS):
            arrived(out_hbm.at[chunk(k)], swap_r.at[2, k])

    for when, copy in pending:
        if when is None:
            copy.wait_send()
        else:
            pl.when(when)(copy.wait_send)


def local(inputs, readout, recept_weight, output_weight, left_vectors, right_vectors, fitness):
    members, seq_len, width = inputs.shape
    full = left_vectors.shape[2]
    rows, half = members * seq_len, full // 2
    step = rows // CHUNKS
    left = left_vectors.reshape(4, full)
    right = right_vectors.reshape(4, width)
    a = jnp.pad(left, ((0, 12), (0, 0)))
    b = jnp.pad(right, ((0, 12), (0, 0)))
    weighted = left_vectors.astype(F32) * fitness[None, :, None]
    weighted = weighted.reshape(4, 16, 2, 128).transpose(1, 2, 0, 3).reshape(16, 8, 128)
    right_tile = right_vectors.reshape(16, 128)
    anywhere = pl.BlockSpec(memory_space=pl.ANY)
    dma = pltpu.SemaphoreType.DMA
    outputs, estimate = pl.pallas_call(
        kernel,
        name="es_step",
        out_shape=(
            jax.ShapeDtypeStruct((rows, width), BF16),
            jax.ShapeDtypeStruct((2, 128, width), F32),
        ),
        in_specs=[anywhere] * 8,
        out_specs=(anywhere, anywhere),
        scratch_shapes=[
            pltpu.VMEM((rows, half), BF16),
            pltpu.VMEM((rows, half), BF16),
            pltpu.VMEM((rows, width), BF16),
            pltpu.VMEM((2, half, width), BF16),
            pltpu.VMEM((2, half, width), BF16),
            pltpu.VMEM((128, half), BF16),
            pltpu.VMEM((16, width), BF16),
            pltpu.VMEM((2 * CHUNKS, step, width + 128), F32),
            pltpu.VMEM((2 * CHUNKS, step, width + 128), F32),
            pltpu.VMEM((rows, width), BF16),
            pltpu.VMEM((4, 4, 8, 128), F32),
            pltpu.VMEM((4, 16, 128), BF16),
            pltpu.VMEM((4, 4, 8, 128), F32),
            pltpu.VMEM((4, 4, 16, 128), BF16),
            pltpu.VMEM((4, 4, 8, 128), F32),
            pltpu.VMEM((4, 4, 16, 128), BF16),
            pltpu.VMEM((2, 128, width), F32),
            dma((CHUNKS, 4)), dma((CHUNKS, 4)), dma((CHUNKS, 4)), dma((CHUNKS, 4)),
            dma((4, CHUNKS)), dma((4, CHUNKS)),
            dma((2, 2, SUBS, 2)), dma((2, 2, SUBS)),
            dma((2, 2, SUBS, 3)), dma((2, 2, SUBS, 3)),
            dma((16,)),
            dma((2 * CHUNKS,)), dma((2 * CHUNKS,)),
            dma((2, 3)), dma((2, 3)), dma((2, 3)), dma((2, 3)),
            dma((2,)), dma((2,)),
        ],
        compiler_params=pltpu.CompilerParams(
            collective_id=0, has_side_effects=True, vmem_limit_bytes=56 * 1024 * 1024
        ),
    )(
        inputs.reshape(rows, width), readout.reshape(rows, width),
        recept_weight, output_weight, a, b, weighted, right_tile,
    )
    return outputs.reshape(members, seq_len, width), estimate


def solution(mesh):
    return jax.shard_map(
        local,
        mesh=mesh,
        in_specs=(
            P("pop", None, "tensor"),
            P("pop", None, "tensor"),
            P(None, "tensor"),
            P(None, "tensor"),
            P(None, "pop", None),
            P(None, "pop", "tensor"),
            P("pop"),
        ),
        out_specs=(P("pop", None, "tensor"), P(None, "pop", "tensor")),
        check_vma=False,
    )
```

time: 353 us -> 147 us (0.42)
  the two profiles are of different devices: /device:TPU:33 before, /device:TPU:1 now
where the time goes in v2:
time: 147 us; the launch traced here: 146 us
  Pallas kernels  136 us (93%)
  local copies, waits for them, and re-layouts  8.71 us (6%)
    pallas_call x1, Pallas kernels, local(): pl.pallas_call(kernel, name='es_step', out_shape=(jax.ShapeDtypeStruct((r...  136 us
    unnamed x2, local copies, waits for them, and re-layouts  3.93 us

profile of v2, /device:TPU:1, one launch (start us, length us, event | category | flops | bytes accessed | tf_op | source)
XLA Modules:
  0.0 146.4 jit_solution(17700955305491138783)
XLA Ops:
  0.6 1.3 reshape.35.r_hbm
  1.9 0.7 reshape.32
  2.6 0.6 pad.9.b_hbm
  3.2 0.8 reshape.31
  4.0 0.8 convert_multiply_fusion
  4.8 0.1 reshape.33
  4.9 0.7 copy.9
  5.6 0.7 pad.8.a_hbm
  6.3 136.2 %es_step.1 = (bf16[768,512]{1,0:T(8,128)(2,1)}, f32[2,128,512]{2,1,0:T(8,128)}) custom-call(bf16[768,512]{1,0:T(8,128)(2,1)} %bitcast.6, bf16[768,512]{1,0:T(8,128)(2,1)} %bitcast.7, bf16[4096,512]{1,0:T(8,128)(2,1)} %wr_hbm.1, bf16[4096,512]{1,0:T(8,128)(2,1)} %wo_hbm.1, bf16[16,4096]{1,0:T(8,128)(2,1)} %pad.8.a_hbm, bf16[16,512]{1,0:T(8,128)(2,1)} %pad.9.b_hbm, ...), custom_call_target="tpu_custom_call" | custom-call | tf_op jit(solution)/shard_map/es_step/pallas_call | solution.py:388
  142.5 2.1 %copy.12 = bf16[2,384,512]{2,1,0:T(8,128)(2,1)} copy(bf16[2,384,512]{2,1,0:T(8,128)(2,1)} %bitcast.8) | data formatting | bytes 1572864
  144.6 1.9 %copy.13 = f32[2,128,512]{2,1,0:T(8,128)} copy(f32[2,128,512]{2,1,0:T(8,128)} %get-tuple-element.9) | data formatting | bytes 1048576

commit v3 on v2

v3 whole, which is shorter than its diff:
```python
import jax
import jax.numpy as jnp
from jax import lax
from jax.experimental import pallas as pl
from jax.experimental.pallas import tpu as pltpu
from jax.sharding import PartitionSpec as P

MESH = pl.DeviceIdType.MESH
noise_scale = 0.02
CHUNKS = 4
SUBS = 4
F32 = jnp.float32
BF16 = jnp.bfloat16


def mod(value, size):
    return lax.rem(value + size, size)


def device(x, y, z, core):
    return ((x * 4 + lax.rem(z, 4)) * 2 + core, (z // 4) * 4 + y)


def kernel(
    x_hbm, ro_hbm, wr_hbm, wo_hbm, left_hbm, right_hbm, fit,
    out_hbm, est_hbm,
    xg, gg, ro, wt, av, bv, proj, part_out, part_in, keep, outs,
    lv, rv, a_own, b_own, l_own, r_own, l1, r1, l2, r2, l3, r3, est,
    xy_s, xy_r, gy_s, gy_r, swap_s, swap_r, wz_s, wz_r, wx_s, wx_r,
    load, part_s, part_r, e1_s, e1_r, e2_s, e2_r, e3_s, e3_r,
):
    pop, tensor = lax.axis_index("pop"), lax.axis_index("tensor")
    x, zl, core = pop // 8, lax.rem(pop // 2, 4), lax.rem(pop, 2)
    zh, y = tensor // 4, lax.rem(tensor, 4)
    z = zh * 4 + zl
    rows, width = ro.shape
    half = xg.shape[1]
    halfquarter = half // 8
    step = rows // CHUNKS
    mover = core != zh
    stays = core == zh

    up, down = device(x, mod(y + 1, 4), z, core), device(x, mod(y + 3, 4), z, core)
    partner = device(x, y, mod(z + 4, 8), 1 - core)
    twin = device(x, y, z, 1 - core)
    z_next = (device(x, y, mod(z + 7, 8), core), device(x, y, mod(z + 1, 8), core))
    x_peer = [device(mod(x + d, 4), y, z, core) for d in range(1, 4)]
    x_up, x_down = x_peer[0], x_peer[2]
    zl_peer = [device(x, y, zh * 4 + mod(zl + d, 4), core) for d in range(1, 4)]
    z_near = [device(x, y, mod(z + d, 8), core) for d in (1, 2, 3, 5, 6, 7)]

    pending = []

    def remote(src, dst, send, recv, target, when=None):
        copy = pltpu.make_async_remote_copy(
            src_ref=src, dst_ref=dst, send_sem=send, recv_sem=recv,
            device_id=target, device_id_type=MESH,
        )
        pending.append((when, copy))
        if when is None:
            copy.start()
        else:
            pl.when(when)(copy.start)

    def arrived(dst, recv):
        pltpu.make_async_remote_copy(
            src_ref=dst, dst_ref=dst, send_sem=recv, recv_sem=recv,
            device_id=twin, device_id_type=MESH,
        ).wait_recv()

    def chunk(k, part=None):
        if part is None:
            return pl.ds(k * step, step)
        return pl.ds(k * step + part * (step // 2), step // 2)

    def columns(which):
        return pl.ds(pl.multiple_of(which * width, width), width)

    mine = columns(y)
    below, above, far = columns(mod(y + 3, 4)), columns(mod(y + 1, 4)), columns(mod(y + 2, 4))
    my_half = pl.ds(pl.multiple_of(core * half, half), half)
    twin_half = pl.ds(pl.multiple_of((1 - core) * half, half), half)

    local = []

    def local_copy(src, dst, sem, when=None):
        copy = pltpu.make_async_copy(src, dst, sem)
        if when is None:
            copy.start()
        else:
            pl.when(when)(copy.start)
        return copy

    load_left = local_copy(left_hbm, lv, load.at[1])
    load_right = local_copy(right_hbm, rv, load.at[2])
    load_x = [
        local_copy(x_hbm.at[chunk(k)], xg.at[chunk(k), mine], load.at[16 + k], stays)
        for k in range(CHUNKS)
    ]
    load_wr = local_copy(wr_hbm.at[my_half], wt.at[zh], load.at[0])
    load_ro = local_copy(ro_hbm, ro, load.at[8], stays)
    load_wo = local_copy(wo_hbm.at[my_half], wt.at[2 + zh], load.at[3])

    barrier = pltpu.get_barrier_semaphore()
    peers = [up, down, partner, twin] + x_peer + z_near
    for peer in peers:
        pl.semaphore_signal(barrier, inc=1, device_id=peer, device_id_type=MESH)

    load_left.wait()
    load_right.wait()
    left = [lv[k].astype(F32) for k in range(2)]
    right = jnp.concatenate([rv[k].astype(F32) for k in range(2)], axis=0)
    full = 2 * half
    for h in range(2):
        cut = [part[:, h * half:(h + 1) * half] for part in left]
        a_own[h] = jnp.concatenate(cut + [jnp.zeros((12, half), F32)], axis=0).astype(BF16)
    b_own[...] = jnp.concatenate([right, jnp.zeros((12, width), F32)], axis=0).astype(BF16)
    r_own[...] = jnp.concatenate(
        [right[:, b * 128:(b + 1) * 128] for b in range(width // 128)], axis=0
    ).astype(BF16)
    member = lax.broadcasted_iota(jnp.int32, (2, full), 0)
    weights = jnp.where(member == 0, fit[0], fit[1])
    weighted = jnp.concatenate([part * weights for part in left], axis=0)
    for q in range(16):
        l_own[q] = jnp.concatenate(
            [weighted[:, (2 * q + c) * 128:(2 * q + c + 1) * 128] for c in range(2)], axis=0
        )
    av[16:, :] = jnp.zeros((av.shape[0] - 16, half), BF16)

    @pl.when(stays)
    def _():
        av[:16, :] = a_own[core]
        bv[...] = b_own[...]

    l1[0] = l_own[pl.ds(4 * x, 4)]
    r1[0] = r_own[...]
    pl.semaphore_wait(barrier, len(peers))

    quarter = half // 4
    sub = quarter // SUBS
    edge = (zl == 0) | (zl == 3)
    inner = (zl == 1) | (zl == 2)
    lag = jnp.where(edge, 0, 1)
    outward = jnp.where(zl == 3, 1, 7)
    z_cross = device(x, y, mod(z + outward, 8), core)
    z_inward = device(x, y, mod(z + 8 - outward, 8), core)

    def piece(n, owner, base=0):
        start = base + owner * quarter + lax.rem(n, SUBS) * sub
        return pl.ds(pl.multiple_of(start, sub), sub)

    def held(n, owner, side):
        return wt.at[(n // SUBS) * 2 + side, piece(n, owner)]

    def weight_start(n):
        remote(
            (wr_hbm, wo_hbm)[n // SUBS].at[piece(n, x, core * half)], held(n, x, zh),
            wz_s.at[n, 0], wz_r.at[n], z_cross, edge,
        )

    def weight_send(place, n, which, target):
        return pltpu.make_async_remote_copy(
            src_ref=place, dst_ref=place, send_sem=wx_s.at[n, which],
            recv_sem=wx_r.at[n, which], device_id=target, device_id_type=MESH,
        )

    def weight_inward(place, n):
        return pltpu.make_async_remote_copy(
            src_ref=place, dst_ref=place, send_sem=wz_s.at[n, 1],
            recv_sem=wz_r.at[n], device_id=z_inward, device_id_type=MESH,
        )

    def weight_slot(slot):
        n = slot - lag

        @pl.when((n >= 0) & (n < 2 * SUBS))
        def _():
            place = held(n, x, 1 - zh)
            arrived(place, wz_r.at[n])
            pl.when(edge)(weight_inward(place, n).start)
            weight_send(place, n, 0, x_up).start()
            weight_send(place, n, 1, x_down).start()

        m = n - 1

        @pl.when((m >= 0) & (m < 2 * SUBS))
        def _():
            odd = lax.rem(m, 2)
            place = held(m, mod(x + 3 - 2 * odd, 4), 1 - zh)
            arrived(place, wx_r.at[m, odd])
            weight_send(place, m, 2, device(mod(x + 1 + 2 * odd, 4), y, z, core)).start()

    def weight_done(w):
        for n in range(w * SUBS, (w + 1) * SUBS):
            odd = n % 2
            arrived(held(n, mod(x + 1 + 2 * odd, 4), 1 - zh), wx_r.at[n, 1 - odd])
            arrived(held(n, mod(x + 2, 4), 1 - zh), wx_r.at[n, 2])

    def weight_sent():
        for n in range(2 * SUBS):
            place = held(n, x, 1 - zh)
            pl.when(edge)(weight_inward(place, n).wait_send)
            for which in range(3):
                weight_send(place, n, which, x_up).wait_send()

    def spread(buf, k, send, recv, when=None):
        place = buf.at[chunk(k), mine]
        remote(place, place, send.at[k, 0], recv.at[k, 0], up, when)
        remote(place, place, send.at[k, 1], recv.at[k, 1], down, when)

    def relay(buf, k, send, recv, when=None):
        def ready(place, sem):
            if when is None:
                arrived(place, sem)
            else:
                pl.when(when)(lambda: arrived(place, sem))

        ready(buf.at[chunk(k), below], recv.at[k, 0])
        place = buf.at[chunk(k, 0), below]
        remote(place, place, send.at[k, 2], recv.at[k, 2], up, when)
        ready(buf.at[chunk(k), above], recv.at[k, 1])
        place = buf.at[chunk(k, 1), above]
        remote(place, place, send.at[k, 3], recv.at[k, 3], down, when)

    def gathered(buf, k, recv):
        arrived(buf.at[chunk(k, 0), far], recv.at[k, 2])
        arrived(buf.at[chunk(k, 1), far], recv.at[k, 3])

    def x_ready(k, when):
        if when is stays:
            pl.when(stays)(load_x[k].wait)
        else:
            pl.when(mover)(lambda: arrived(xg.at[chunk(k), mine], swap_r.at[0, k]))
        spread(xg, k, xy_s, xy_r, when)

    def part(which, buf, k, side, sender, fresh):
        slot = which * CHUNKS + k
        value = buf[chunk(k), :]
        product = jnp.dot(value, wt[2 * which + side], preferred_element_type=F32)
        if fresh:
            proj[which, chunk(k), :] = lax.dot_general(
                value, av[...], (((1,), (1,)), ((), ())), preferred_element_type=F32
            )
        send = pltpu.make_async_remote_copy(
            src_ref=part_out.at[slot], dst_ref=part_in.at[slot],
            send_sem=part_s.at[slot], recv_sem=part_r.at[slot],
            device_id=twin, device_id_type=MESH,
        )
        pending.append((sender, send))

        @pl.when(sender)
        def _():
            part_out[slot, :, :width] = product
            part_out[slot, :, width:] = proj[which, chunk(k), :]
            send.start()

        @pl.when(jnp.logical_not(sender))
        def _():
            keep[slot] = product

    def total(which, k):
        at = which * 2 + k // (CHUNKS // 2)
        slot = which * CHUNKS + k
        arrived(part_in.at[slot], part_r.at[slot])
        scaled = noise_scale * (proj[which, chunk(k), :] + part_in[slot, :, width:])
        return (
            keep[slot] + part_in[slot, :, :width]
            + scaled[:, at:at + 1] * bv[at:at + 1, :].astype(F32)
        )

    def gate(k):
        gated = jax.nn.sigmoid(total(0, k)) * ro[chunk(k), :].astype(F32)
        gg[chunk(k), mine] = gated.astype(BF16)

    def a_part(k):
        gathered(xg, k, xy_r)
        if k == 0:
            load_wr.wait()
        part(0, xg, k, zh, mover, True)

    def a_finish(k):
        @pl.when(stays)
        def _():
            if k == 0:
                load_ro.wait()
            gate(k)

        spread(gg, k, gy_s, gy_r, stays)

    def b_part(k):
        part(0, xg, k, 1 - zh, stays, False)

    def b_finish(k):
        @pl.when(mover)
        def _():
            arrived(ro.at[chunk(k)], swap_r.at[1, k])
            gate(k)

        spread(gg, k, gy_s, gy_r, mover)

    store = []

    def c_part(k):
        gathered(gg, k, gy_r)
        part(1, gg, k, 1 - zh, stays, True)

    def c_finish(k):
        @pl.when(mover)
        def _():
            outs[chunk(k), :] = total(1, k).astype(BF16)

        remote(
            outs.at[chunk(k)], out_hbm.at[chunk(k)],
            swap_s.at[2, k], swap_r.at[2, k], partner, mover,
        )

    def d_part(k):
        part(1, gg, k, zh, mover, False)

    def d_finish(k):
        @pl.when(stays)
        def _():
            outs[chunk(k), :] = total(1, k).astype(BF16)

        store.append(local_copy(outs.at[chunk(k)], out_hbm.at[chunk(k)], load.at[16 + CHUNKS + k], stays))

    def estimate_one():
        for d in range(3):
            remote(
                l_own.at[pl.ds(4 * mod(x + d + 1, 4), 4)], l1.at[d + 1],
                e1_s.at[0, d], e1_r.at[0, d], x_peer[d],
            )
            remote(r_own, r1.at[d + 1], e1_s.at[1, d], e1_r.at[1, d], x_peer[d])

    def estimate_two():
        for d in range(3):
            arrived(l1.at[d + 1], e1_r.at[0, d])
            arrived(r1.at[d + 1], e1_r.at[1, d])
        for d in range(3):
            remote(
                l1.at[:, mod(zl + d + 1, 4)], l2.at[d + 1],
                e2_s.at[0, d], e2_r.at[0, d], zl_peer[d],
            )
            remote(r1, r2.at[d + 1], e2_s.at[1, d], e2_r.at[1, d], zl_peer[d])
        l2[0] = l1[:, zl]
        r2[0] = r1[...]

    def estimate_three():
        for d in range(3):
            arrived(l2.at[d + 1], e2_r.at[0, d])
            arrived(r2.at[d + 1], e2_r.at[1, d])
        remote(l2, l3, e3_s.at[0], e3_r.at[0], twin)
        remote(r2, r3, e3_s.at[1], e3_r.at[1], twin)

    def estimate_sum():
        arrived(l3, e3_r.at[0])
        arrived(r3, e3_r.at[1])
        n = 16
        lrow = lax.broadcasted_iota(jnp.int32, (n * 8, n * 16), 0)
        rrow = lax.broadcasted_iota(jnp.int32, (n * 8, n * 16), 1)
        same = (lrow // 8 == rrow // 16) & (lrow % 8 == core * 4 + rrow % 4)
        pick = jnp.where(same, 1.0, 0.0).astype(BF16)
        block = (lax.broadcasted_iota(jnp.int32, (n * 16, 128), 0) % 16) // 4
        which = (lax.broadcasted_iota(jnp.int32, (n * 8, width), 0) // 2) % 2
        sums = [None, None]
        for left, right in ((l2, r2), (l3, r3)):
            lt = left[...].reshape(n * 8, 128).T
            rt = right[...].reshape(n * 16, 128).astype(F32)
            wide = jnp.concatenate(
                [jnp.where(block == b, rt, 0.0).astype(BF16) for b in range(width // 128)], axis=1
            )
            chosen = jnp.dot(pick, wide, preferred_element_type=F32)
            high = lt.astype(BF16)
            rest = lt - high.astype(F32)
            middle = rest.astype(BF16)
            low = (rest - middle.astype(F32)).astype(BF16)
            for k in range(2):
                operand = jnp.where(which == k, chosen, 0.0).astype(BF16)
                for piece in (low, middle, high):
                    term = jnp.dot(piece, operand, preferred_element_type=F32)
                    sums[k] = term if sums[k] is None else sums[k] + term
        for k in range(2):
            est[k] = sums[k]
        store.append(local_copy(est, est_hbm, load.at[15]))

    def x_swap(k):
        remote(
            x_hbm.at[chunk(k)], xg.at[chunk(k), mine],
            swap_s.at[0, k], swap_r.at[0, k], partner, mover,
        )

    def ro_swap(k):
        remote(
            ro_hbm.at[chunk(k)], ro.at[chunk(k)],
            swap_s.at[1, k], swap_r.at[1, k], partner, mover,
        )

    def x_relay(k, when):
        relay(xg, k, xy_s, xy_r, when)

    def g_relay(k, when):
        relay(gg, k, gy_s, gy_r, when)

    x_ready(0, stays)
    weight_start(0)
    weight_start(1)
    x_swap(0)
    weight_start(2)
    x_relay(0, stays)
    x_ready(1, stays)

    remote(b_own, bv, swap_s.at[3, 0], swap_r.at[3, 0], partner, mover)
    remote(
        a_own.at[1 - core], av.at[pl.ds(0, 16)],
        swap_s.at[3, 1], swap_r.at[3, 1], twin, stays,
    )
    estimate_one()
    weight_slot(0)
    weight_start(3)
    weight_start(4)
    x_ready(2, stays)
    x_relay(1, stays)
    x_swap(1)
    x_ready(0, mover)
    x_ready(3, stays)
    weight_slot(1)
    x_relay(0, mover)
    weight_start(5)
    x_swap(2)
    weight_start(6)
    x_ready(1, mover)
    weight_slot(2)

    @pl.when(mover)
    def _():
        arrived(av.at[pl.ds(0, 16)], swap_r.at[3, 1])
        arrived(bv, swap_r.at[3, 0])

    a_part(0)
    x_swap(3)
    x_relay(1, mover)
    ro_swap(0)
    estimate_two()
    weight_slot(3)
    x_ready(2, mover)
    a_part(1)
    x_relay(2, stays)
    weight_slot(4)
    ro_swap(1)
    a_finish(0)
    weight_start(7)
    x_relay(2, mover)
    weight_slot(5)
    x_ready(3, mover)
    a_part(2)
    x_relay(3, stays)
    weight_done(0)
    b_part(0)
    estimate_three()
    weight_slot(6)
    x_relay(3, mover)
    b_finish(0)
    a_part(3)
    g_relay(0, stays)
    a_finish(1)
    a_finish(2)
    weight_slot(7)
    b_part(1)
    b_part(2)
    ro_swap(2)
    g_relay(0, mover)
    b_part(3)
    weight_slot(8)
    b_finish(1)
    g_relay(1, stays)
    a_finish(3)
    g_relay(2, stays)
    weight_slot(9)
    ro_swap(3)
    b_finish(2)
    load_wo.wait()
    weight_done(1)
    estimate_sum()
    c_part(0)
    g_relay(1, mover)
    c_finish(0)
    d_part(0)
    g_relay(2, mover)
    b_finish(3)
    c_part(1)
    g_relay(3, stays)
    c_finish(1)
    c_part(2)
    d_part(1)
    g_relay(3, mover)
    d_finish(0)
    c_finish(2)
    d_part(2)
    c_part(3)
    d_finish(1)
    d_finish(2)
    d_part(3)
    c_finish(3)
    d_finish(3)

    for copy in store[:1]:
        copy.wait()

    @pl.when(stays)
    def _():
        for copy in store[1:]:
            copy.wait()

    @pl.when(mover)
    def _():
        for k in range(CHUNKS):
            arrived(out_hbm.at[chunk(k)], swap_r.at[2, k])

    weight_sent()
    for when, copy in pending:
        if when is None:
            copy.wait_send()
        else:
            pl.when(when)(copy.wait_send)


def local(inputs, readout, recept_weight, output_weight, left_vectors, right_vectors, fitness):
    members, seq_len, width = inputs.shape
    full = left_vectors.shape[2]
    rows, half = members * seq_len, full // 2
    step = rows // CHUNKS
    anywhere = pl.BlockSpec(memory_space=pl.ANY)
    dma = pltpu.SemaphoreType.DMA
    outputs, estimate = pl.pallas_call(
        kernel,
        name="es_step",
        out_shape=(
            jax.ShapeDtypeStruct((rows, width), BF16),
            jax.ShapeDtypeStruct((2, 128, width), F32),
        ),
        in_specs=[anywhere] * 6 + [pl.BlockSpec(memory_space=pltpu.SMEM)],
        out_specs=(anywhere, anywhere),
        scratch_shapes=[
            pltpu.VMEM((rows, half), BF16),
            pltpu.VMEM((rows, half), BF16),
            pltpu.VMEM((rows, width), BF16),
            pltpu.VMEM((4, half, width), BF16),
            pltpu.VMEM((128, half), BF16),
            pltpu.VMEM((16, width), BF16),
            pltpu.VMEM((2, rows, 128), F32),
            pltpu.VMEM((2 * CHUNKS, step, width + 128), F32),
            pltpu.VMEM((2 * CHUNKS, step, width + 128), F32),
            pltpu.VMEM((2 * CHUNKS, step, width), F32),
            pltpu.VMEM((rows, width), BF16),
            pltpu.VMEM((2, members, full), BF16),
            pltpu.VMEM((2, members, width), BF16),
            pltpu.VMEM((2, 16, half), BF16),
            pltpu.VMEM((16, width), BF16),
            pltpu.VMEM((16, 8, 128), F32),
            pltpu.VMEM((16, 128), BF16),
            pltpu.VMEM((4, 4, 8, 128), F32),
            pltpu.VMEM((4, 16, 128), BF16),
            pltpu.VMEM((4, 4, 8, 128), F32),
            pltpu.VMEM((4, 4, 16, 128), BF16),
            pltpu.VMEM((4, 4, 8, 128), F32),
            pltpu.VMEM((4, 4, 16, 128), BF16),
            pltpu.VMEM((2, 128, width), F32),
            dma((CHUNKS, 4)), dma((CHUNKS, 4)), dma((CHUNKS, 4)), dma((CHUNKS, 4)),
            dma((4, CHUNKS)), dma((4, CHUNKS)),
            dma((2 * SUBS, 2)), dma((2 * SUBS,)),
            dma((2 * SUBS, 3)), dma((2 * SUBS, 3)),
            dma((16 + 2 * CHUNKS,)),
            dma((2 * CHUNKS,)), dma((2 * CHUNKS,)),
            dma((2, 3)), dma((2, 3)), dma((2, 3)), dma((2, 3)),
            dma((2,)), dma((2,)),
        ],
        compiler_params=pltpu.CompilerParams(
            collective_id=0, has_side_effects=True, vmem_limit_bytes=56 * 1024 * 1024
        ),
    )(
        inputs.reshape(rows, width), readout.reshape(rows, width),
        recept_weight, output_weight, left_vectors, right_vectors, fitness,
    )
    return outputs.reshape(members, seq_len, width), estimate * (1.0 / (noise_scale * 64))


def solution(mesh):
    return jax.shard_map(
        local,
        mesh=mesh,
        in_specs=(
            P("pop", None, "tensor"),
            P("pop", None, "tensor"),
            P(None, "tensor"),
            P(None, "tensor"),
            P(None, "pop", None),
            P(None, "pop", "tensor"),
            P("pop"),
        ),
        out_specs=(P("pop", None, "tensor"), P(None, "pop", "tensor")),
        check_vma=False,
    )
```

time: 147 us -> 112 us (0.76)
  the two profiles are of different devices: /device:TPU:1 before, /device:TPU:33 now
where the time goes in v3:
time: 112 us
  Pallas kernels  107 us (96%)
  local copies, waits for them, and re-layouts  2.06 us (2%)
  other arithmetic  1.88 us (2%)
    pallas_call x1, Pallas kernels, local(): pl.pallas_call(kernel, name='es_step', out_shape=(jax.ShapeDtypeStruct((r...  107 us

profile of v3, /device:TPU:33, one launch (start us, length us, event | category | flops | bytes accessed | tf_op | source)
XLA Modules:
  0.0 111.8 jit_solution(13881051034438474347)
XLA Ops:
  0.6 107.2 %es_step.1 = (bf16[768,512]{1,0:T(8,128)(2,1)}, f32[2,128,512]{2,1,0:T(8,128)}) custom-call(bf16[768,512]{1,0:T(8,128)(2,1)} %bitcast.3, bf16[768,512]{1,0:T(8,128)(2,1)} %bitcast.4, bf16[4096,512]{1,0:T(8,128)(2,1)} %wr_hbm.1, bf16[4096,512]{1,0:T(8,128)(2,1)} %wo_hbm.1, bf16[2,2,4096]{2,1,0:T(2,128)(2,1)} %left_hbm.1, bf16[2,2,512]{2,1,0:T(2,128)(2,1)} %right_hbm.1, ...), custom_call_target="tpu_custom_call" | custom-call | tf_op jit(solution)/shard_map/es_step/pallas_call | solution.py:534
  107.8 1.9 %broadcast_multiply_fusion = f32[2,128,512]{2,1,0:T(8,128)} fusion(f32[2,128,512]{2,1,0:T(8,128)} %get-tuple-element.5), kind=kLoop, calls=%fused_computation | loop fusion | flops 131072 | bytes 1048576 | tf_op jit(solution)/shard_map/mul | solution.py:584
  109.7 2.1 %copy.10 = bf16[2,384,512]{2,1,0:T(8,128)(2,1)} copy(bf16[2,384,512]{2,1,0:T(8,128)(2,1)} %bitcast.5) | data formatting | bytes 1572864

commit v4 on v3

--- a/solution.py
+++ b/solution.py
@@ -181,7 +181,7 @@
             weight_send(place, n, 0, x_up).start()
             weight_send(place, n, 1, x_down).start()
 
-        m = n - 1
+        m = n - 2
 
         @pl.when((m >= 0) & (m < 2 * SUBS))
         def _():
@@ -402,12 +402,17 @@
         relay(gg, k, gy_s, gy_r, when)
 
     x_ready(0, stays)
+    x_relay(0, stays)
+    x_swap(0)
     weight_start(0)
+    x_ready(1, stays)
     weight_start(1)
-    x_swap(0)
+    x_swap(1)
+    x_ready(0, mover)
     weight_start(2)
-    x_relay(0, stays)
-    x_ready(1, stays)
+    weight_start(3)
+    x_ready(2, stays)
+    x_relay(1, stays)
 
     remote(b_own, bv, swap_s.at[3, 0], swap_r.at[3, 0], partner, mover)
     remote(
@@ -416,20 +421,13 @@
     )
     estimate_one()
     weight_slot(0)
-    weight_start(3)
+    x_swap(2)
     weight_start(4)
-    x_ready(2, stays)
-    x_relay(1, stays)
-    x_swap(1)
-    x_ready(0, mover)
+    x_relay(2, stays)
     x_ready(3, stays)
-    weight_slot(1)
     x_relay(0, mover)
     weight_start(5)
-    x_swap(2)
-    weight_start(6)
-    x_ready(1, mover)
-    weight_slot(2)
+    weight_slot(1)
 
     @pl.when(mover)
     def _():
@@ -437,70 +435,73 @@
         arrived(bv, swap_r.at[3, 0])
 
     a_part(0)
-    x_swap(3)
-    x_relay(1, mover)
-    ro_swap(0)
+    weight_slot(2)
+    x_ready(1, mover)
     estimate_two()
     weight_slot(3)
+    weight_start(6)
     x_ready(2, mover)
-    a_part(1)
-    x_relay(2, stays)
+    x_relay(1, mover)
+    x_swap(3)
+    a_finish(0)
     weight_slot(4)
-    ro_swap(1)
-    a_finish(0)
-    weight_start(7)
     x_relay(2, mover)
     weight_slot(5)
-    x_ready(3, mover)
-    a_part(2)
-    x_relay(3, stays)
-    weight_done(0)
-    b_part(0)
     estimate_three()
     weight_slot(6)
+    a_part(1)
+    weight_start(7)
+    a_finish(1)
+    x_ready(3, mover)
+    g_relay(0, stays)
+    ro_swap(0)
+    weight_done(0)
+    x_relay(3, stays)
+    weight_slot(7)
     x_relay(3, mover)
+    b_part(0)
+    g_relay(1, stays)
+    ro_swap(1)
+    a_part(2)
+    b_part(1)
+    weight_slot(8)
+    a_finish(2)
+    a_part(3)
+    b_part(2)
     b_finish(0)
-    a_part(3)
-    g_relay(0, stays)
-    a_finish(1)
-    a_finish(2)
-    weight_slot(7)
-    b_part(1)
-    b_part(2)
     ro_swap(2)
+    ro_swap(3)
+    weight_slot(9)
+    b_finish(1)
+    weight_slot(10)
     g_relay(0, mover)
     b_part(3)
-    weight_slot(8)
-    b_finish(1)
-    g_relay(1, stays)
-    a_finish(3)
+    g_relay(1, mover)
     g_relay(2, stays)
-    weight_slot(9)
-    ro_swap(3)
-    b_finish(2)
     load_wo.wait()
     weight_done(1)
+    b_finish(2)
     estimate_sum()
     c_part(0)
-    g_relay(1, mover)
     c_finish(0)
-    d_part(0)
-    g_relay(2, mover)
+    a_finish(3)
     b_finish(3)
     c_part(1)
     g_relay(3, stays)
     c_finish(1)
+    d_part(0)
+    g_relay(2, mover)
+    g_relay(3, mover)
+    d_part(1)
     c_part(2)
-    d_part(1)
-    g_relay(3, mover)
     d_finish(0)
     c_finish(2)
     d_part(2)
     c_part(3)
+    c_finish(3)
+    d_part(3)
     d_finish(1)
     d_finish(2)
-    d_part(3)
-    c_finish(3)
     d_finish(3)
 
     for copy in store[:1]:

time: 112 us -> 108 us (0.964)
  Pallas kernels: 107 us -> 103 us
    pallas_call x1, Pallas kernels: 107 us -> 103 us  [local(): pl.pallas_call(kernel, name='es_step', out_shape=(jax.ShapeDtypeStruct((r...]
where the time goes in v4:
time: 108 us
  Pallas kernels  103 us (95%)
  local copies, waits for them, and re-layouts  2.06 us (2%)
  other arithmetic  1.88 us (2%)
    pallas_call x1, Pallas kernels, local(): pl.pallas_call(kernel, name='es_step', out_shape=(jax.ShapeDtypeStruct((r...  103 us

profile of v4, /device:TPU:33, one launch (start us, length us, event | category | flops | bytes accessed | tf_op | source)
XLA Modules:
  0.0 107.8 jit_solution(16080640590942705827)
XLA Ops:
  0.6 103.2 %es_step.1 = (bf16[768,512]{1,0:T(8,128)(2,1)}, f32[2,128,512]{2,1,0:T(8,128)}) custom-call(bf16[768,512]{1,0:T(8,128)(2,1)} %bitcast.3, bf16[768,512]{1,0:T(8,128)(2,1)} %bitcast.4, bf16[4096,512]{1,0:T(8,128)(2,1)} %wr_hbm.1, bf16[4096,512]{1,0:T(8,128)(2,1)} %wo_hbm.1, bf16[2,2,4096]{2,1,0:T(2,128)(2,1)} %left_hbm.1, bf16[2,2,512]{2,1,0:T(2,128)(2,1)} %right_hbm.1, ...), custom_call_target="tpu_custom_call" | custom-call | tf_op jit(solution)/shard_map/es_step/pallas_call | solution.py:535
  103.8 1.9 %broadcast_multiply_fusion = f32[2,128,512]{2,1,0:T(8,128)} fusion(f32[2,128,512]{2,1,0:T(8,128)} %get-tuple-element.5), kind=kLoop, calls=%fused_computation | loop fusion | flops 131072 | bytes 1048576 | tf_op jit(solution)/shard_map/mul | solution.py:585
  105.7 2.1 %copy.10 = bf16[2,384,512]{2,1,0:T(8,128)(2,1)} copy(bf16[2,384,512]{2,1,0:T(8,128)(2,1)} %bitcast.5) | data formatting | bytes 1572864

commit v5 on v4

--- a/solution.py
+++ b/solution.py
@@ -455,20 +455,20 @@
     x_ready(3, mover)
     g_relay(0, stays)
     ro_swap(0)
+    ro_swap(1)
     weight_done(0)
     x_relay(3, stays)
     weight_slot(7)
     x_relay(3, mover)
     b_part(0)
     g_relay(1, stays)
-    ro_swap(1)
     a_part(2)
     b_part(1)
+    b_finish(0)
     weight_slot(8)
     a_finish(2)
     a_part(3)
     b_part(2)
-    b_finish(0)
     ro_swap(2)
     ro_swap(3)
     weight_slot(9)

time: 108 us -> 107 us (level)
  no operation moved by 1% of the time
where the time goes in v5:
time: 107 us
  Pallas kernels  102 us (95%)
  local copies, waits for them, and re-layouts  2.06 us (2%)
  other arithmetic  1.88 us (2%)
    pallas_call x1, Pallas kernels, local(): pl.pallas_call(kernel, name='es_step', out_shape=(jax.ShapeDtypeStruct((r...  102 us

profile of v5, /device:TPU:33, one launch (start us, length us, event | category | flops | bytes accessed | tf_op | source)
XLA Modules:
  0.0 106.9 jit_solution(5051539805829200689)
XLA Ops:
  0.6 102.3 %es_step.1 = (bf16[768,512]{1,0:T(8,128)(2,1)}, f32[2,128,512]{2,1,0:T(8,128)}) custom-call(bf16[768,512]{1,0:T(8,128)(2,1)} %bitcast.3, bf16[768,512]{1,0:T(8,128)(2,1)} %bitcast.4, bf16[4096,512]{1,0:T(8,128)(2,1)} %wr_hbm.1, bf16[4096,512]{1,0:T(8,128)(2,1)} %wo_hbm.1, bf16[2,2,4096]{2,1,0:T(2,128)(2,1)} %left_hbm.1, bf16[2,2,512]{2,1,0:T(2,128)(2,1)} %right_hbm.1, ...), custom_call_target="tpu_custom_call" | custom-call | tf_op jit(solution)/shard_map/es_step/pallas_call | solution.py:535
  103.0 1.9 %broadcast_multiply_fusion = f32[2,128,512]{2,1,0:T(8,128)} fusion(f32[2,128,512]{2,1,0:T(8,128)} %get-tuple-element.5), kind=kLoop, calls=%fused_computation | loop fusion | flops 131072 | bytes 1048576 | tf_op jit(solution)/shard_map/mul | solution.py:585
  104.8 2.1 %copy.10 = bf16[2,384,512]{2,1,0:T(8,128)(2,1)} copy(bf16[2,384,512]{2,1,0:T(8,128)(2,1)} %bitcast.5) | data formatting | bytes 1572864

commit v6 on v5

--- a/solution.py
+++ b/solution.py
@@ -469,12 +469,12 @@
     a_finish(2)
     a_part(3)
     b_part(2)
+    b_finish(1)
     ro_swap(2)
     ro_swap(3)
     weight_slot(9)
-    b_finish(1)
+    g_relay(0, mover)
     weight_slot(10)
-    g_relay(0, mover)
     b_part(3)
     g_relay(1, mover)
     g_relay(2, stays)

time: 107 us -> 107 us (level)
  no operation moved by 1% of the time
where the time goes in v6:
time: 107 us
  Pallas kernels  102 us (95%)
  local copies, waits for them, and re-layouts  2.06 us (2%)
  other arithmetic  1.88 us (2%)
    pallas_call x1, Pallas kernels, local(): pl.pallas_call(kernel, name='es_step', out_shape=(jax.ShapeDtypeStruct((r...  102 us

profile of v6, /device:TPU:33, one launch (start us, length us, event | category | flops | bytes accessed | tf_op | source)
XLA Modules:
  0.0 106.9 jit_solution(17646238158550273916)
XLA Ops:
  0.6 102.3 %es_step.1 = (bf16[768,512]{1,0:T(8,128)(2,1)}, f32[2,128,512]{2,1,0:T(8,128)}) custom-call(bf16[768,512]{1,0:T(8,128)(2,1)} %bitcast.3, bf16[768,512]{1,0:T(8,128)(2,1)} %bitcast.4, bf16[4096,512]{1,0:T(8,128)(2,1)} %wr_hbm.1, bf16[4096,512]{1,0:T(8,128)(2,1)} %wo_hbm.1, bf16[2,2,4096]{2,1,0:T(2,128)(2,1)} %left_hbm.1, bf16[2,2,512]{2,1,0:T(2,128)(2,1)} %right_hbm.1, ...), custom_call_target="tpu_custom_call" | custom-call | tf_op jit(solution)/shard_map/es_step/pallas_call | solution.py:535
  102.9 1.9 %broadcast_multiply_fusion = f32[2,128,512]{2,1,0:T(8,128)} fusion(f32[2,128,512]{2,1,0:T(8,128)} %get-tuple-element.5), kind=kLoop, calls=%fused_computation | loop fusion | flops 131072 | bytes 1048576 | tf_op jit(solution)/shard_map/mul | solution.py:585
  104.8 2.1 %copy.10 = bf16[2,384,512]{2,1,0:T(8,128)(2,1)} copy(bf16[2,384,512]{2,1,0:T(8,128)(2,1)} %bitcast.5) | data formatting | bytes 1572864
